TPU v7x, 128 devices: a whole 4x4x4 slice. The times are simulated.
128 devices in a mesh: dp: 64 (over z, y, x_lo, core), seq: 2 (over x_hi).
Axes of the slice: x: 4 (x_hi: 2, x_lo: 2; x = x_hi * 2 + x_lo), y: 4, z: 4, core: 2. Of those that a mesh axis runs over, the one named last changes fastest.
Arguments:
- tokens: bfloat16 [16384, 896], P(('dp', 'seq')), may hold values from -6 to 6
- doc_ids: int32 [64, 256], P('dp'), may hold values from 0 to 3, as said below
- selected: int32 [16384], P(('dp', 'seq')), may hold values 0 or 1
- groups: int32 [16384], P(('dp', 'seq')), may hold values from 0 to 2
- group_weight: float32 [3], replicated, may hold values from 0.5 to 2
- w_q: bfloat16 [896, 896], P(('dp', 'seq')), may hold values from -0.1875 to 0.1875
- w_k: bfloat16 [896, 128], P(('dp', 'seq')), may hold values from -0.1875 to 0.1875
- w_v: bfloat16 [896, 128], P(('dp', 'seq')), may hold values from -0.1875 to 0.1875
- b_q: bfloat16 [896], P(('dp', 'seq')), may hold values from -3 to 3
- b_k: bfloat16 [128], P(('dp', 'seq')), may hold values from -3 to 3
- b_v: bfloat16 [128], P(('dp', 'seq')), may hold values from -3 to 3
- w_o: bfloat16 [896, 896], P(('dp', 'seq')), may hold values from -0.75 to 0.75
- gain_attn: bfloat16 [896], P(('dp', 'seq')), may hold values from 0.5 to 1.5
- w_gate: bfloat16 [896, 4864], P(('dp', 'seq')), may hold values from -0.1875 to 0.1875
- w_up: bfloat16 [896, 4864], P(('dp', 'seq')), may hold values from -0.1875 to 0.1875
- w_down: bfloat16 [4864, 896], P(('dp', 'seq')), may hold values from -0.078125 to 0.078125
- gain_ffn: bfloat16 [896], P(('dp', 'seq')), may hold values from 0.5 to 1.5
- cotangent: bfloat16 [16384, 896], P(('dp', 'seq')), may hold values from -24 to 24
Outputs:
- mixed_out: bfloat16 [16384, 896], P(('dp', 'seq'))
- input_grad: float32 [16384, 896], P(('dp', 'seq'))
- grad_w_q: float32 [896, 896], P(('dp', 'seq'))
- grad_w_k: float32 [896, 128], P(('dp', 'seq'))
- grad_w_v: float32 [896, 128], P(('dp', 'seq'))
- grad_b_q: float32 [896], P(('dp', 'seq'))
- grad_b_k: float32 [128], replicated
- grad_b_v: float32 [128], P(('dp', 'seq'))
- grad_w_o: float32 [896, 896], P(('dp', 'seq'))
- grad_gain_attn: float32 [896], P(('dp', 'seq'))
- grad_w_gate: float32 [896, 4864], P(('dp', 'seq'))
- grad_w_up: float32 [896, 4864], P(('dp', 'seq'))
- grad_w_down: float32 [4864, 896], P(('dp', 'seq'))
- grad_gain_ffn: float32 [896], P(('dp', 'seq'))
Inputs may be any that keep to these rules, and one draw needn't show every extreme that they name: `doc_ids`: within each sequence the numbers never fall and start at 0; document 2 holds at least the places 256 // 4 to 191.
All inputs are finite; a program needn't handle non-finite values. No bound on the sum of `selected` on one device may be relied on, other than what follows from the above.
Results may differ from a plain program's by a relative error of at most 0.02.
Values may be sent and summed in bfloat16 or wider, within the bound.
No kernel may reach another device: no remote copies, remote signals or barrier semaphores. Data moves between devices by JAX's collectives and lax.ppermute only.
A program may use at most 192 MiB of HBM per device.

v0:
```python
import jax
import jax.numpy as jnp
from jax import lax
from jax.sharding import PartitionSpec as P

HEADS = 14
KV_HEADS = 2
HEAD = 64


EPSILON = 1e-05
MASKED = -1e30


def passed_along(array, axis, by):
    count = lax.axis_size(axis)
    pairs = [(i, i + by) for i in range(count) if 0 <= i + by < count]
    return lax.ppermute(array, axis, pairs)


def angles(row_start, row_count):
    place = (row_start + jnp.arange(row_count, dtype=jnp.int32)).astype(jnp.float32)
    freq = 10000.0 ** (-jnp.arange(0, HEAD, 2, dtype=jnp.int32).astype(jnp.float32) / HEAD)
    turn = place[:, None] * freq[None, :]
    turn = jnp.concatenate([turn, turn], -1)
    return (jnp.cos(turn)[:, None, :], jnp.sin(turn)[:, None, :])


def rotate(value, cos_table, sin_table):
    half = value.shape[-1] // 2
    swapped = jnp.concatenate([-value[..., half:], value[..., :half]], -1)
    return value * cos_table + swapped * sin_table


def matmul(left, right):
    return jnp.dot(left, right, preferred_element_type=jnp.float32)


def norm_back(value, inverse, gain, grad_normed):
    grad_gain = jnp.sum(grad_normed * value * inverse, 0)
    scaled = grad_normed * gain
    cube = inverse * inverse * inverse
    grad_value = inverse * scaled - value * cube * jnp.mean(scaled * value, -1, keepdims=True)
    return (grad_value, grad_gain)


def shards(
    tokens,
    doc_ids,
    selected,
    groups,
    group_weight,
    w_q,
    w_k,
    w_v,
    b_q,
    b_k,
    b_v,
    w_o,
    gain_attn,
    w_gate,
    w_up,
    w_down,
    gain_ffn,
    cotangent,
):
    row_count = tokens.shape[0]
    feature = tokens.shape[1]
    kv_width = KV_HEADS * HEAD
    per_group = HEADS // KV_HEADS
    row_start = lax.axis_index("seq") * row_count
    full_q, full_k, full_v, full_bq, full_bk, full_bv, full_o, full_g1 = (
        lax.all_gather(w_q, ("dp", "seq"), axis=0, tiled=True),
        lax.all_gather(w_k, ("dp", "seq"), axis=0, tiled=True),
        lax.all_gather(w_v, ("dp", "seq"), axis=0, tiled=True),
        lax.all_gather(b_q, ("dp", "seq"), axis=0, tiled=True),
        lax.all_gather(b_k, ("dp", "seq"), axis=0, tiled=True),
        lax.all_gather(b_v, ("dp", "seq"), axis=0, tiled=True),
        lax.all_gather(w_o, ("dp", "seq"), axis=0, tiled=True),
        lax.all_gather(gain_attn, ("dp", "seq"), axis=0, tiled=True),
    )
    full_gate, full_up, full_down, full_g2 = (
        lax.all_gather(w_gate, ("dp", "seq"), axis=0, tiled=True),
        lax.all_gather(w_up, ("dp", "seq"), axis=0, tiled=True),
        lax.all_gather(w_down, ("dp", "seq"), axis=0, tiled=True),
        lax.all_gather(gain_ffn, ("dp", "seq"), axis=0, tiled=True),
    )
    cos_table, sin_table = angles(row_start, row_count)
    source = tokens.astype(jnp.float32)
    inv_one = lax.rsqrt(jnp.mean(source * source, -1, keepdims=True) + EPSILON)
    normed_one = (source * inv_one * full_g1.astype(jnp.float32)).astype(jnp.bfloat16)
    query_raw = matmul(normed_one, full_q) + full_bq.astype(jnp.float32)[None, :]
    queries = rotate(query_raw.reshape(row_count, HEADS, HEAD), cos_table, sin_table).astype(
        jnp.bfloat16
    )
    key_raw = matmul(normed_one, full_k) + full_bk.astype(jnp.float32)[None, :]
    key_own = rotate(key_raw.reshape(row_count, KV_HEADS, HEAD), cos_table, sin_table)
    key_own = key_own.astype(jnp.bfloat16).reshape(row_count, kv_width)
    value_own = (matmul(normed_one, full_v) + full_bv.astype(jnp.float32)[None, :]).astype(
        jnp.bfloat16
    )
    key_prev, value_prev = passed_along((key_own, value_own), "seq", 1)
    all_keys = jnp.concatenate([key_prev, key_own], 0).reshape(2 * row_count, KV_HEADS, HEAD)
    all_values = jnp.concatenate([value_prev, value_own], 0).reshape(2 * row_count, KV_HEADS, HEAD)
    seq_ids = doc_ids[0]
    padded = jnp.concatenate([jnp.full((row_count,), -1, jnp.int32), seq_ids])
    key_ids = lax.dynamic_slice_in_dim(padded, row_start, 2 * row_count)
    query_ids = lax.dynamic_slice_in_dim(seq_ids, row_start, row_count)
    query_place = row_start + jnp.arange(row_count, dtype=jnp.int32)
    key_place = row_start - row_count + jnp.arange(2 * row_count, dtype=jnp.int32)
    allowed = (key_ids[None, :] == query_ids[:, None]) & (
        key_place[None, :] <= query_place[:, None]
    )
    heads_q = queries.reshape(row_count, KV_HEADS, per_group, HEAD)
    score = (
        jnp.einsum("qgjd,kgd->gjqk", heads_q, all_keys, preferred_element_type=jnp.float32) * 0.125
    )
    score = jnp.where(allowed, score, MASKED)
    row_top = jnp.max(score, -1, keepdims=True)
    exponent = jnp.exp(score - row_top)
    soft_weights = exponent / jnp.sum(exponent, -1, keepdims=True)
    soft_low = soft_weights.astype(jnp.bfloat16)
    attended = jnp.einsum(
        "gjqk,kgd->qgjd", soft_low, all_values, preferred_element_type=jnp.float32
    )
    mixed_heads = attended.reshape(row_count, feature).astype(jnp.bfloat16)
    resid = source + matmul(mixed_heads, full_o)
    inv_two = lax.rsqrt(jnp.mean(resid * resid, -1, keepdims=True) + EPSILON)
    normed_two = (resid * inv_two * full_g2.astype(jnp.float32)).astype(jnp.bfloat16)
    gate_part = matmul(normed_two, full_gate)
    up_part = matmul(normed_two, full_up)
    hidden = (jax.nn.silu(gate_part) * up_part).astype(jnp.bfloat16)
    output = resid + matmul(hidden, full_down)
    mixed_out = output.astype(jnp.bfloat16)
    onehot = (
        groups[:, None] == jnp.arange(group_weight.shape[0], dtype=jnp.int32)[None, :]
    ).astype(jnp.float32)
    row_weight = selected.astype(jnp.float32) * jnp.sum(onehot * group_weight[None, :], -1)
    grad_output = cotangent.astype(jnp.float32) * row_weight[:, None]
    grad_low = grad_output.astype(jnp.bfloat16)
    back_gate, back_up, back_down, back_g2 = (
        lax.all_gather(w_gate, ("dp", "seq"), axis=0, tiled=True),
        lax.all_gather(w_up, ("dp", "seq"), axis=0, tiled=True),
        lax.all_gather(w_down, ("dp", "seq"), axis=0, tiled=True),
        lax.all_gather(gain_ffn, ("dp", "seq"), axis=0, tiled=True),
    )
    grad_hidden = matmul(grad_low, back_down.T)
    sigmoid_gate = jax.nn.sigmoid(gate_part)
    grad_gate = (
        grad_hidden * up_part * sigmoid_gate * (1.0 + gate_part * (1.0 - sigmoid_gate))
    ).astype(jnp.bfloat16)
    grad_up = (grad_hidden * gate_part * sigmoid_gate).astype(jnp.bfloat16)
    grad_normed_two = matmul(grad_gate, back_gate.T) + matmul(grad_up, back_up.T)
    grad_resid_norm, grad_g2 = norm_back(
        resid, inv_two, back_g2.astype(jnp.float32), grad_normed_two
    )
    grad_resid = grad_output + grad_resid_norm
    grad_down_w = matmul(hidden.T, grad_low)
    grad_gate_w = matmul(normed_two.T, grad_gate)
    grad_up_w = matmul(normed_two.T, grad_up)
    ffn_sums = (
        lax.psum_scatter(grad_gate_w, ("dp", "seq"), scatter_dimension=0, tiled=True),
        lax.psum_scatter(grad_up_w, ("dp", "seq"), scatter_dimension=0, tiled=True),
        lax.psum_scatter(grad_down_w, ("dp", "seq"), scatter_dimension=0, tiled=True),
        lax.psum_scatter(grad_g2, ("dp", "seq"), scatter_dimension=0, tiled=True),
    )
    back_q, back_k, back_v, back_bq, back_bk, back_bv, back_o, back_g1 = (
        lax.all_gather(w_q, ("dp", "seq"), axis=0, tiled=True),
        lax.all_gather(w_k, ("dp", "seq"), axis=0, tiled=True),
        lax.all_gather(w_v, ("dp", "seq"), axis=0, tiled=True),
        lax.all_gather(b_q, ("dp", "seq"), axis=0, tiled=True),
        lax.all_gather(b_k, ("dp", "seq"), axis=0, tiled=True),
        lax.all_gather(b_v, ("dp", "seq"), axis=0, tiled=True),
        lax.all_gather(w_o, ("dp", "seq"), axis=0, tiled=True),
        lax.all_gather(gain_attn, ("dp", "seq"), axis=0, tiled=True),
    )
    grad_attn = grad_resid.astype(jnp.bfloat16)
    grad_o_w = matmul(mixed_heads.T, grad_attn)
    grad_mixed = (
        matmul(grad_attn, back_o.T)
        .astype(jnp.bfloat16)
        .reshape(row_count, KV_HEADS, per_group, HEAD)
    )
    grad_soft = jnp.einsum(
        "qgjd,kgd->gjqk", grad_mixed, all_values, preferred_element_type=jnp.float32
    )
    row_centre = jnp.sum(soft_weights * grad_soft, -1, keepdims=True)
    grad_score = (soft_weights * (grad_soft - row_centre)).astype(jnp.bfloat16)
    grad_query = (
        jnp.einsum("gjqk,kgd->qgjd", grad_score, all_keys, preferred_element_type=jnp.float32)
        * 0.125
    )
    grad_keys = (
        jnp.einsum("gjqk,qgjd->kgd", grad_score, heads_q, preferred_element_type=jnp.float32)
        * 0.125
    )
    grad_values = jnp.einsum(
        "gjqk,qgjd->kgd", soft_low, grad_mixed, preferred_element_type=jnp.float32
    )
    grad_keys = grad_keys.reshape(2 * row_count, kv_width)
    grad_values = grad_values.reshape(2 * row_count, kv_width)
    back_key, back_value = (
        passed_along(grad_keys[:row_count].astype(jnp.bfloat16), "seq", -1).astype(jnp.float32),
        passed_along(grad_values[:row_count].astype(jnp.bfloat16), "seq", -1).astype(jnp.float32),
    )
    key_total = grad_keys[row_count:] + back_key
    value_total = grad_values[row_count:] + back_value
    grad_q_raw = (
        rotate(grad_query.reshape(row_count, HEADS, HEAD), cos_table, -sin_table)
        .reshape(row_count, feature)
        .astype(jnp.bfloat16)
    )
    grad_k_raw = (
        rotate(key_total.reshape(row_count, KV_HEADS, HEAD), cos_table, -sin_table)
        .reshape(row_count, kv_width)
        .astype(jnp.bfloat16)
    )
    grad_v_raw = value_total.astype(jnp.bfloat16)
    grad_k_bias = lax.psum(jnp.sum(grad_k_raw.astype(jnp.float32), 0), ("dp", "seq"))
    grad_q_w = matmul(normed_one.T, grad_q_raw)
    grad_k_w = matmul(normed_one.T, grad_k_raw)
    grad_v_w = matmul(normed_one.T, grad_v_raw)
    grad_q_bias = jnp.sum(grad_q_raw.astype(jnp.float32), 0)
    grad_v_bias = jnp.sum(grad_v_raw.astype(jnp.float32), 0)
    grad_normed_one = (
        matmul(grad_q_raw, back_q.T) + matmul(grad_k_raw, back_k.T) + matmul(grad_v_raw, back_v.T)
    )
    grad_source_norm, grad_g1 = norm_back(
        source, inv_one, back_g1.astype(jnp.float32), grad_normed_one
    )
    input_grad = grad_resid + grad_source_norm
    attn_sums = (
        lax.psum_scatter(grad_q_w, ("dp", "seq"), scatter_dimension=0, tiled=True),
        lax.psum_scatter(grad_k_w, ("dp", "seq"), scatter_dimension=0, tiled=True),
        lax.psum_scatter(grad_v_w, ("dp", "seq"), scatter_dimension=0, tiled=True),
        lax.psum_scatter(grad_q_bias, ("dp", "seq"), scatter_dimension=0, tiled=True),
        lax.psum_scatter(grad_v_bias, ("dp", "seq"), scatter_dimension=0, tiled=True),
        lax.psum_scatter(grad_o_w, ("dp", "seq"), scatter_dimension=0, tiled=True),
        lax.psum_scatter(grad_g1, ("dp", "seq"), scatter_dimension=0, tiled=True),
    )
    return (
        mixed_out,
        input_grad,
        attn_sums[0],
        attn_sums[1],
        attn_sums[2],
        attn_sums[3],
        grad_k_bias,
        attn_sums[4],
        attn_sums[5],
        attn_sums[6],
        ffn_sums[0],
        ffn_sums[1],
        ffn_sums[2],
        ffn_sums[3],
    )


def solution(mesh):
    in_specs = (
        P(("dp", "seq"), None),
        P("dp", None),
        P(("dp", "seq")),
        P(("dp", "seq")),
        P(),
        P(("dp", "seq"), None),
        P(("dp", "seq"), None),
        P(("dp", "seq"), None),
        P(("dp", "seq")),
        P(("dp", "seq")),
        P(("dp", "seq")),
        P(("dp", "seq"), None),
        P(("dp", "seq")),
        P(("dp", "seq"), None),
        P(("dp", "seq"), None),
        P(("dp", "seq"), None),
        P(("dp", "seq")),
        P(("dp", "seq"), None),
    )
    out_specs = (
        P(("dp", "seq"), None),
        P(("dp", "seq"), None),
        P(("dp", "seq"), None),
        P(("dp", "seq"), None),
        P(("dp", "seq"), None),
        P(("dp", "seq")),
        P(),
        P(("dp", "seq")),
        P(("dp", "seq"), None),
        P(("dp", "seq")),
        P(("dp", "seq"), None),
        P(("dp", "seq"), None),
        P(("dp", "seq"), None),
        P(("dp", "seq")),
    )
    return jax.shard_map(shards, mesh=mesh, in_specs=in_specs, out_specs=out_specs, check_vma=False)
```

profile of v0, /device:TPU:0, one launch (start us, length us, event | category | flops | bytes accessed | tf_op | source)
XLA Modules:
  0.0 3588.7 jit_solution(10678165792681287173)
XLA Ops:
  14.7 68.4 %all-reduce.22 = (bf16[128]{0:T(256)(128)(2,1)S(1)}, bf16[896]{0:T(1024)(128)(2,1)S(1)}, bf16[896]{0:T(1024)(128)(2,1)S(1)}, bf16[128]{0:T(256)(128)(2,1)S(1)}, bf16[896]{0:T(1024)(128)(2,1)S(1)}) all-reduce(bf16[128]{0:T(256)(128)(2,1)S(1)} %dynamic-update-slice.1, ...), channel_id=1, replica_groups=mesh['dp'=64,'seq'=2] {'dp','seq'}, use_global_device_ids=true, to_apply=%add.2 | all-reduce | flops 2944 | bytes 11776
  83.1 313.5 %all-gather.1 = bf16[128,7,128]{2,1,0:T(8,128)(2,1)S(1)} all-gather(bf16[1,7,128]{2,1,0:T(8,128)(2,1)} %bitcast.198), channel_id=1, replica_groups=mesh['dp'=64,'seq'=2] {'dp','seq'}, dimensions={0}, use_global_device_ids=true | all-gather | bytes 231168 | tf_op jit(solution)/shard_map/all_gather | solution.py:74
  404.2 311.3 %all-gather = bf16[128,7,128]{2,1,0:T(8,128)(2,1)S(1)} all-gather(bf16[1,7,128]{2,1,0:T(8,128)(2,1)S(1)} %bitcast.199), channel_id=1, replica_groups=mesh['dp'=64,'seq'=2] {'dp','seq'}, dimensions={0}, use_global_device_ids=true | all-gather | bytes 231168 | tf_op jit(solution)/shard_map/all_gather | solution.py:75
  715.9 5.8 collective-permute-start
  736.0 196.8 %all-gather.17.cloned.1.call-done = bf16[128,7,4864]{2,1,0:T(8,128)(2,1)} async-done(((bf16[1,7,4864]{2,1,0:T(8,128)(2,1)}), bf16[128,7,4864]{2,1,0:T(8,128)(2,1)}) %all-gather.17.cloned.1.call-update) | async-done | bytes 8716304 | tf_op jit(solution)/shard_map/all_gather | solution.py:83
  932.8 13.5 reshape.246
  946.3 305.5 %all-gather.19.cloned.1.call-done = bf16[128,7,4864]{2,1,0:T(8,128)(2,1)} async-done(((bf16[1,7,4864]{2,1,0:T(8,128)(2,1)}), bf16[128,7,4864]{2,1,0:T(8,128)(2,1)}) %all-gather.19.cloned.1.call-update) | async-done | bytes 8716304 | tf_op jit(solution)/shard_map/all_gather | solution.py:84
  1251.8 13.5 reshape.248
  1265.3 6.5 fusion.69
  1274.8 294.8 %all-gather.21.cloned.1.call-done = bf16[128,38,896]{2,1,0:T(8,128)(2,1)} async-done(((bf16[1,38,896]{2,1,0:T(8,128)(2,1)}), bf16[128,38,896]{2,1,0:T(8,128)(2,1)}) %all-gather.21.cloned.1.call-update) | async-done | bytes 8716304 | tf_op jit(solution)/shard_map/all_gather | solution.py:85
  1569.7 13.0 reshape.250
  1582.6 10.8 multiply_convert_fusion
  1593.4 7.2 fusion.70
  1616.3 8.5 fusion.73
  1624.8 8.4 fusion.72
  1633.2 934.5 %fusion.64 = (f32[8,4864]{1,0:T(8,128)S(1)}, f32[8,4864]{1,0:T(8,128)S(1)}) fusion(f32[896,4864]{1,0:T(8,128)} %fusion.72, f32[896,4864]{1,0:T(8,128)} %fusion.73), kind=kCustom, calls=%all-reduce-scatter.3 | all-reduce-scatter fusion | flops 9961473 | bytes 35176448
  2579.6 7.4 fusion.35
  2587.0 573.4 %fusion.2 = f32[48,896]{1,0:T(8,128)} fusion(f32[4864,896]{1,0:T(8,128)} %fusion.35), kind=kCustom, calls=%all-reduce-scatter.2 | all-reduce-scatter fusion | flops 5505025 | bytes 17604608
  3189.1 14.4 collective-permute-start.9
  3208.5 6.4 collective-permute-start.6
  3220.4 11.3 collective-permute-start.34
  3237.8 7.8 collective-permute-start.30
  3245.6 5.8 collective-permute-start.29
  3251.4 6.2 fusion.8
  3297.9 7.5 collective-permute-start.58
  3311.5 64.5 %all-reduce.20 = (f32[896]{0:T(1024)S(1)}, f32[128]{0:T(128)}, f32[128]{0:T(128)S(1)}, f32[896]{0:T(1024)S(1)}, f32[896]{0:T(1024)S(1)}) all-reduce(f32[896]{0:T(1024)S(1)} %reduce_sum.118, f32[128]{0:T(128)S(1)} %get-tuple-element.38, f32[128]{0:T(128)S(1)} %get-tuple-element.36, ...), channel_id=5, replica_groups=mesh['dp'=64,'seq'=2] {'dp','seq'}, use_global_device_ids=true, to_apply=%region_12.13.clone | all-reduce | flops 2944 | bytes 23552
  3420.0 30.3 concatenate.60
  3450.2 13.3 collective-permute-start.45
  3468.3 8.3 collective-permute-start.42
  3479.2 30.3 concatenate.61
  3513.9 6.7 collective-permute-start.38
  3529.1 45.2 %concatenate.62 = f32[1318,896]{1,0:T(8,128)} concatenate(f32[22,896]{1,0:T(8,128)} %copy-done.56, f32[48,896]{1,0:T(8,128)S(1)} %copy-done.29, f32[48,896]{1,0:T(8,128)S(1)} %copy-done.31, f32[48,896]{1,0:T(8,128)S(1)} %copy-done.33, f32[48,896]{1,0:T(8,128)} %copy-done.34, f32[48,896]{1,0:T(8,128)} %copy-done.35, f32[48,896]{1,0:T(8,128)} %copy-done.36, f32[48,896]{1,0:T(8,128)} %copy-done.37, ...), dimensions={0} | concatenate | bytes 9447424
  (387 shorter events, 220.7 us)
Async XLA Ops:
  7.2 716.0 %all-gather.13.cloned.1.call-start = ((), (), s32[]{:S(2)}) async-start(), calls=%async_computation | async-start | bytes 1849344 | tf_op jit(solution)/shard_map/all_gather | solution.py:73
  7.9 718.8 %all-gather.15.cloned.1.call-start = ((), (), s32[]{:S(2)}) async-start(), calls=%async_computation.1 | async-start | bytes 1849344 | tf_op jit(solution)/shard_map/all_gather | solution.py:79
  8.7 924.1 %all-gather.17.cloned.1.call-start = ((), (), s32[]{:S(2)}) async-start(), calls=%async_computation.2 | async-start | bytes 10039296 | tf_op jit(solution)/shard_map/all_gather | solution.py:83
  9.4 1242.4 %all-gather.19.cloned.1.call-start = ((), (), s32[]{:S(2)}) async-start(), calls=%async_computation.3 | async-start | bytes 10039296 | tf_op jit(solution)/shard_map/all_gather | solution.py:84
  10.0 1559.7 %all-gather.21.cloned.1.call-start = ((), (), s32[]{:S(2)}) async-start(), calls=%async_computation.4 | async-start | bytes 9246720 | tf_op jit(solution)/shard_map/all_gather | solution.py:85
  10.6 3565.4 %all-reduce.26.cloned.1.call-start = ((), (), s32[]{:S(2)}) async-start(), calls=%async_computation.5 | async-start | bytes 14680064
  400.4 330.0 %collective-permute-start.1 = (bf16[128,128]{0,1:T(8,128)(2,1)S(1)}, bf16[128,128]{0,1:T(8,128)(2,1)S(1)}, u32[]{:S(2)}, u32[]{:S(2)}) collective-permute-start(bf16[128,128]{0,1:T(8,128)(2,1)S(1)} %fusion.40), channel_id=1, source_target_pairs={{0,1},{2,3},{4,5},{6,7},{8,9},{10,11},{12,13},{14,15},{16,17},{18,... | collective-permute-start | bytes 98312 | tf_op jit(solution)/shard_map/ppermute | solution.py:18
  2568.4 606.2 %collective-permute-start.18 = (f32[8,4864]{1,0:T(8,128)S(1)}, f32[8,4864]{1,0:T(8,128)}, u32[]{:S(2)}, u32[]{:S(2)}) collective-permute-start(f32[8,4864]{1,0:T(8,128)S(1)} %get-tuple-element.34), channel_id=1, source_target_pairs={{0,15},{1,16},{2,17},{3,18},{4,19},{5,20},{6,21},{7,22},{8,23},{9,... | collective-permute-start | bytes 466952
  2570.3 607.4 %collective-permute-start.17 = (f32[8,4864]{1,0:T(8,128)S(1)}, f32[8,4864]{1,0:T(8,128)}, u32[]{:S(2)}, u32[]{:S(2)}) collective-permute-start(f32[8,4864]{1,0:T(8,128)S(1)} %get-tuple-element.34), channel_id=1, source_target_pairs={{0,14},{1,15},{2,16},{3,17},{4,18},{5,19},{6,20},{7,21},{8,22},{9,... | collective-permute-start | bytes 466952
  2572.3 590.3 %collective-permute-start.3 = (bf16[128,128]{0,1:T(8,128)(2,1)}, bf16[128,128]{0,1:T(8,128)(2,1)S(1)}, u32[]{:S(2)}, u32[]{:S(2)}) collective-permute-start(bf16[128,128]{0,1:T(8,128)(2,1)} %bitcast.48), channel_id=1, source_target_pairs={{1,0},{3,2},{5,4},{7,6},{9,8},{11,10},{13,12},{15,14},{17,16},{19,... | collective-permute-start | bytes 98312 | tf_op jit(solution)/shard_map/ppermute | solution.py:18
  2573.6 593.0 %collective-permute-start.2 = (bf16[128,128]{0,1:T(8,128)(2,1)}, bf16[128,128]{0,1:T(8,128)(2,1)}, u32[]{:S(2)}, u32[]{:S(2)}) collective-permute-start(bf16[128,128]{0,1:T(8,128)(2,1)} %bitcast.40), channel_id=1, source_target_pairs={{1,0},{3,2},{5,4},{7,6},{9,8},{11,10},{13,12},{15,14},{17,16},{19,... | collective-permute-start | bytes 98312 | tf_op jit(solution)/shard_map/ppermute | solution.py:18
  3174.7 28.8 collective-permute-start.13
  3177.8 28.5 collective-permute-start.12
  3179.1 29.4 collective-permute-start.11
  3184.3 30.7 collective-permute-start.10
  3237.8 29.0 collective-permute-start.30
  3272.5 36.5 %collective-permute-start.61 = (f32[48,896]{1,0:T(8,128)}, f32[48,896]{1,0:T(8,128)S(1)}, u32[]{:S(2)}, u32[]{:S(2)}) collective-permute-start(f32[48,896]{1,0:T(8,128)} %fusion.2), channel_id=1, source_target_pairs={{0,26},{1,27},{2,28},{3,29},{4,30},{5,31},{6,32},{7,33},{8,34},{9,... | collective-permute-start | bytes 516104
  3295.1 83.2 %collective-permute-start.60 = (f32[48,896]{1,0:T(8,128)}, f32[48,896]{1,0:T(8,128)S(1)}, u32[]{:S(2)}, u32[]{:S(2)}) collective-permute-start(f32[48,896]{1,0:T(8,128)} %fusion.2), channel_id=1, source_target_pairs={{0,25},{1,26},{2,27},{3,28},{4,29},{5,30},{6,31},{7,32},{8,33},{9,... | collective-permute-start | bytes 516104
  3296.4 86.1 %collective-permute-start.59 = (f32[48,896]{1,0:T(8,128)}, f32[48,896]{1,0:T(8,128)S(1)}, u32[]{:S(2)}, u32[]{:S(2)}) collective-permute-start(f32[48,896]{1,0:T(8,128)} %fusion.2), channel_id=1, source_target_pairs={{0,24},{1,25},{2,26},{3,27},{4,28},{5,29},{6,30},{7,31},{8,32},{9,... | collective-permute-start | bytes 516104
  3297.9 89.6 %collective-permute-start.58 = (f32[48,896]{1,0:T(8,128)}, f32[48,896]{1,0:T(8,128)S(1)}, u32[]{:S(2)}, u32[]{:S(2)}) collective-permute-start(f32[48,896]{1,0:T(8,128)} %fusion.2), channel_id=1, source_target_pairs={{0,23},{1,24},{2,25},{3,26},{4,27},{5,28},{6,29},{7,30},{8,31},{9,... | collective-permute-start | bytes 516104
  3305.4 84.7 %collective-permute-start.57 = (f32[48,896]{1,0:T(8,128)}, f32[48,896]{1,0:T(8,128)S(1)}, u32[]{:S(2)}, u32[]{:S(2)}) collective-permute-start(f32[48,896]{1,0:T(8,128)} %fusion.2), channel_id=1, source_target_pairs={{0,22},{1,23},{2,24},{3,25},{4,26},{5,27},{6,28},{7,29},{8,30},{9,... | collective-permute-start | bytes 516104
  3309.8 85.9 %collective-permute-start.56 = (f32[48,896]{1,0:T(8,128)}, f32[48,896]{1,0:T(8,128)S(1)}, u32[]{:S(2)}, u32[]{:S(2)}) collective-permute-start(f32[48,896]{1,0:T(8,128)} %fusion.2), channel_id=1, source_target_pairs={{0,21},{1,22},{2,23},{3,24},{4,25},{5,26},{6,27},{7,28},{8,29},{9,... | collective-permute-start | bytes 516104
  3400.4 49.8 %collective-permute-start.50 = (f32[48,896]{1,0:T(8,128)}, f32[48,896]{1,0:T(8,128)}, u32[]{:S(2)}, u32[]{:S(2)}) collective-permute-start(f32[48,896]{1,0:T(8,128)} %fusion.2), channel_id=1, source_target_pairs={{0,15},{1,16},{2,17},{3,18},{4,19},{5,20},{6,21},{7,22},{8,23},{9,... | collective-permute-start | bytes 516104
  3402.7 60.8 %collective-permute-start.49 = (f32[48,896]{1,0:T(8,128)}, f32[48,896]{1,0:T(8,128)}, u32[]{:S(2)}, u32[]{:S(2)}) collective-permute-start(f32[48,896]{1,0:T(8,128)} %fusion.2), channel_id=1, source_target_pairs={{0,14},{1,15},{2,16},{3,17},{4,18},{5,19},{6,20},{7,21},{8,22},{9,... | collective-permute-start | bytes 516104
  3408.1 57.4 %collective-permute-start.48 = (f32[48,896]{1,0:T(8,128)}, f32[48,896]{1,0:T(8,128)}, u32[]{:S(2)}, u32[]{:S(2)}) collective-permute-start(f32[48,896]{1,0:T(8,128)} %fusion.2), channel_id=1, source_target_pairs={{0,13},{1,14},{2,15},{3,16},{4,17},{5,18},{6,19},{7,20},{8,21},{9,... | collective-permute-start | bytes 516104
  3411.4 56.9 %collective-permute-start.47 = (f32[48,896]{1,0:T(8,128)}, f32[48,896]{1,0:T(8,128)}, u32[]{:S(2)}, u32[]{:S(2)}) collective-permute-start(f32[48,896]{1,0:T(8,128)} %fusion.2), channel_id=1, source_target_pairs={{0,12},{1,13},{2,14},{3,15},{4,16},{5,17},{6,18},{7,19},{8,20},{9,... | collective-permute-start | bytes 516104
  3414.6 62.0 %collective-permute-start.46 = (f32[48,896]{1,0:T(8,128)}, f32[48,896]{1,0:T(8,128)}, u32[]{:S(2)}, u32[]{:S(2)}) collective-permute-start(f32[48,896]{1,0:T(8,128)} %fusion.2), channel_id=1, source_target_pairs={{0,11},{1,12},{2,13},{3,14},{4,15},{5,16},{6,17},{7,18},{8,19},{9,... | collective-permute-start | bytes 516104
  3450.2 59.3 %collective-permute-start.45 = (f32[48,896]{1,0:T(8,128)}, f32[48,896]{1,0:T(8,128)}, u32[]{:S(2)}, u32[]{:S(2)}) collective-permute-start(f32[48,896]{1,0:T(8,128)} %fusion.2), channel_id=1, source_target_pairs={{0,10},{1,11},{2,12},{3,13},{4,14},{5,15},{6,16},{7,17},{8,18},{9,... | collective-permute-start | bytes 516104
  3463.5 48.5 %collective-permute-start.44 = (f32[48,896]{1,0:T(8,128)}, f32[48,896]{1,0:T(8,128)}, u32[]{:S(2)}, u32[]{:S(2)}) collective-permute-start(f32[48,896]{1,0:T(8,128)} %fusion.2), channel_id=1, source_target_pairs={{0,9},{1,10},{2,11},{3,12},{4,13},{5,14},{6,15},{7,16},{8,17},{9,1... | collective-permute-start | bytes 516104
  3465.5 48.4 %collective-permute-start.43 = (f32[48,896]{1,0:T(8,128)}, f32[48,896]{1,0:T(8,128)}, u32[]{:S(2)}, u32[]{:S(2)}) collective-permute-start(f32[48,896]{1,0:T(8,128)} %fusion.2), channel_id=1, source_target_pairs={{0,8},{1,9},{2,10},{3,11},{4,12},{5,13},{6,14},{7,15},{8,16},{9,17... | collective-permute-start | bytes 516104
  3468.3 52.3 %collective-permute-start.42 = (f32[48,896]{1,0:T(8,128)}, f32[48,896]{1,0:T(8,128)}, u32[]{:S(2)}, u32[]{:S(2)}) collective-permute-start(f32[48,896]{1,0:T(8,128)} %fusion.2), channel_id=1, source_target_pairs={{0,7},{1,8},{2,9},{3,10},{4,11},{5,12},{6,13},{7,14},{8,15},{9,16}... | collective-permute-start | bytes 516104
  3476.6 46.0 %collective-permute-start.41 = (f32[48,896]{1,0:T(8,128)}, f32[48,896]{1,0:T(8,128)}, u32[]{:S(2)}, u32[]{:S(2)}) collective-permute-start(f32[48,896]{1,0:T(8,128)} %fusion.2), channel_id=1, source_target_pairs={{0,6},{1,7},{2,8},{3,9},{4,10},{5,11},{6,12},{7,13},{8,14},{9,15},... | collective-permute-start | bytes 516104
  (118 other events, 11198.7 us)
Sparse Core Ops, SparseCore 0:
  9.7 301.3 all-gather.12
  312.8 300.2 all-gather.14
  614.8 317.8 all-gather.16
  934.3 317.4 all-gather.18
  1253.4 316.2 all-gather.20
  3177.9 265.5 all-reduce.25
where the time goes:
time: 3600 us; the launch traced here: 3590 us
  blocking collectives  2270 us (63%)
  waiting for transfers between devices  807 us (22%)
  starting transfers between devices  234 us (6%)
  local copies, waits for them, and re-layouts  172 us (5%)
  matrix products  83.2 us (2%)
    unnamed x4, blocking collectives  1640 us
    all_gather x1, blocking collectives, shards(): lax.all_gather(w_k, ('dp', 'seq'), axis=0, tiled=True)  313 us
    all_gather x1, blocking collectives, shards(): lax.all_gather(w_v, ('dp', 'seq'), axis=0, tiled=True)  311 us
    all_gather x1, waiting for transfers between devices, shards(): lax.all_gather(w_up, ('dp', 'seq'), axis=0, tiled=True)  305 us
    all_gather x1, waiting for transfers between devices, shards(): lax.all_gather(w_down, ('dp', 'seq'), axis=0, tiled=True)  295 us
    unnamed x60, starting transfers between devices  221 us
    all_gather x1, waiting for transfers between devices, shards(): lax.all_gather(w_gate, ('dp', 'seq'), axis=0, tiled=True)  197 us
    unnamed x192, local copies, waits for them, and re-layouts  169 us
  transfers between devices with their start and end apart: 69, of which 6 were waited for; matrix products, arithmetic and copies ran while one was open for 21% of the time, Pallas kernels for 0%

commit v1 on v0

v1 whole, which is shorter than its diff:
```python
import jax
import jax.numpy as jnp
from jax import lax
from jax.sharding import Mesh
from jax.sharding import PartitionSpec as P

HEADS = 14
KV_HEADS = 2
HEAD = 64
GROUP = HEADS // KV_HEADS
D = 896
FF = 4864
ROWS = 7
UNIT = 38
UNIT_PAD = 40
LOCAL_FF = 16 * UNIT_PAD
QW = GROUP * HEAD
BLOCK = QW + 2 * HEAD

EPSILON = 1e-05
MASKED = -1e30
f32 = jnp.float32
bf16 = jnp.bfloat16

ALL = ("z", "y", "xl", "c", "xh")
TEAM = ("xl", "c", "xh")
RING = ("xh", "xl", "c")
PLANE = ("z", "y")
SAME_CORE = ("z", "y", "xl", "xh")
SWAP = [(0, 1), (1, 0)]


def matmul(left, right):
    return jnp.dot(left, right, preferred_element_type=f32)


def matmul_nt(left, right):
    return lax.dot_general(left, right, (((1,), (1,)), ((), ())), preferred_element_type=f32)


def matmul_tn(left, right):
    return lax.dot_general(left, right, (((0,), (0,)), ((), ())), preferred_element_type=f32)


def exchange(array, axes):
    return lax.all_to_all(array, axes, split_axis=0, concat_axis=0, tiled=True)


def angles(count):
    place = jnp.arange(count, dtype=jnp.int32).astype(f32)
    freq = 10000.0 ** (-jnp.arange(0, HEAD, 2, dtype=jnp.int32).astype(f32) / HEAD)
    turn = place[:, None] * freq[None, :]
    turn = jnp.concatenate([turn, turn], -1)
    return (jnp.cos(turn)[:, None, :], jnp.sin(turn)[:, None, :])


def rotate(value, cos_table, sin_table):
    half = value.shape[-1] // 2
    swapped = jnp.concatenate([-value[..., half:], value[..., :half]], -1)
    return value * cos_table + swapped * sin_table


def inverse_rms(value):
    return lax.rsqrt(jnp.mean(value * value, -1, keepdims=True) + EPSILON)


def norm_back(value, inverse, gain, grad_normed):
    scaled = grad_normed * gain
    cube = inverse * inverse * inverse
    return inverse * scaled - value * cube * jnp.mean(scaled * value, -1, keepdims=True)


def in_order(own, other, first):
    return jnp.where(first, jnp.concatenate([own, other], 0), jnp.concatenate([other, own], 0))


def by_team(weight):
    parts = weight.reshape(ROWS, 16, 8, UNIT)
    parts = jnp.pad(parts, ((0, 0), (0, 0), (0, 0), (0, UNIT_PAD - UNIT)))
    return parts.transpose(2, 0, 1, 3).reshape(8, ROWS, LOCAL_FF)


def from_team(grad):
    parts = grad.reshape(8, ROWS, 16, UNIT_PAD)[..., :UNIT]
    return parts.transpose(1, 2, 0, 3).reshape(ROWS, FF)


def shards(
    tokens,
    doc_ids,
    selected,
    groups,
    group_weight,
    w_q,
    w_k,
    w_v,
    b_q,
    b_k,
    b_v,
    w_o,
    gain_attn,
    w_gate,
    w_up,
    w_down,
    gain_ffn,
    cotangent,
):
    xl, core, xh = lax.axis_index("xl"), lax.axis_index("c"), lax.axis_index("xh")
    team_index = (xl * 2 + core) * 2 + xh
    first = xh == 0
    row_count = tokens.shape[0]

    small = jnp.concatenate([b_q, b_k, b_v, gain_attn, gain_ffn])
    small = jnp.pad(small, (0, BLOCK - small.shape[0]))[None, :]
    halves = []
    for g in range(KV_HEADS):
        part = jnp.concatenate(
            [
                w_q[:, g * QW : (g + 1) * QW],
                w_k[:, g * HEAD : (g + 1) * HEAD],
                w_v[:, g * HEAD : (g + 1) * HEAD],
            ],
            1,
        )
        halves.append(jnp.concatenate([part, small], 0))
    send = jnp.broadcast_to(jnp.stack(halves)[None], (32, 2, 8, BLOCK)).reshape(64, 8, BLOCK)
    from_core = exchange(send, SAME_CORE)
    from_other = lax.ppermute(from_core, "c", SWAP)
    blocks = jnp.concatenate([from_core, from_other], 0)

    slot = jnp.arange(1024, dtype=jnp.int32)
    block, row = slot // 8, slot % 8
    relation, place = block // 64, block % 64
    source_core = jnp.where(relation == 0, core, 1 - core)
    owner = (place // 2 * 2 + source_core) * 2 + place % 2
    feature = jnp.where(row < ROWS, owner * ROWS + row, -1)
    spread = (jnp.arange(D, dtype=jnp.int32)[:, None] == feature[None, :]).astype(bf16)

    w_qkv = matmul(spread, blocks.reshape(1024, BLOCK)).astype(bf16)
    small_all = blocks[:, ROWS, :32].reshape(2, 32, 2, 32)
    small_all = jnp.where(core == 0, small_all, small_all[::-1])
    small_all = small_all.transpose(1, 0, 2, 3).reshape(128, 32).astype(f32)
    full_bq = small_all[:, 0:7].reshape(D)
    full_bk = small_all[:, 7]
    full_bv = small_all[:, 8]
    full_g1 = small_all[:, 9:16].reshape(D)
    full_g2 = small_all[:, 16:23].reshape(D)
    bias = jnp.concatenate(
        [
            lax.dynamic_slice_in_dim(full_bq, xh * QW, QW),
            lax.dynamic_slice_in_dim(full_bk, xh * HEAD, HEAD),
            lax.dynamic_slice_in_dim(full_bv, xh * HEAD, HEAD),
        ]
    )

    onehot = (
        groups[:, None] == jnp.arange(group_weight.shape[0], dtype=jnp.int32)[None, :]
    ).astype(f32)
    row_weight = selected.astype(f32) * jnp.sum(onehot * group_weight[None, :], -1)
    grad_output = cotangent.astype(f32) * row_weight[:, None]
    grad_low = grad_output.astype(bf16)
    both = jnp.concatenate([tokens, grad_low], 1)
    both_team = lax.all_gather(both, RING, axis=0, tiled=False)
    both_team = both_team.reshape(2, 2, 2, row_count, 2 * D).transpose(1, 2, 0, 3, 4)
    both_team = both_team.reshape(8 * row_count, 2 * D)
    tokens_team, grad_low_team = both_team[:, :D], both_team[:, D:]

    wide = jnp.concatenate(
        [by_team(w_gate), by_team(w_up), jnp.broadcast_to(w_o[None], (8, ROWS, D))], 2
    )
    wide = exchange(wide, TEAM).reshape(8 * ROWS, 2 * LOCAL_FF + D)
    wide = lax.all_gather(wide, PLANE, axis=0, tiled=True)
    gate_up = wide[:, : 2 * LOCAL_FF]
    full_o = wide[:, 2 * LOCAL_FF :]
    down = jnp.pad(w_down, ((0, UNIT_PAD - UNIT), (0, 0)))
    down = lax.all_gather(down, PLANE, axis=0, tiled=True)

    tokens_seq = in_order(tokens, lax.ppermute(tokens, "xh", SWAP), first)
    length = tokens_seq.shape[0]
    source = tokens_seq.astype(f32)
    inv_one = inverse_rms(source)
    normed_one = (source * inv_one * full_g1[None, :]).astype(bf16)
    raw = matmul(normed_one, w_qkv) + bias[None, :]
    cos_table, sin_table = angles(length)
    queries = rotate(raw[:, :QW].reshape(length, GROUP, HEAD), cos_table, sin_table).astype(bf16)
    keys = rotate(raw[:, QW : QW + HEAD], cos_table[:, 0], sin_table[:, 0]).astype(bf16)
    values = raw[:, QW + HEAD :].astype(bf16)
    ids = doc_ids[0]
    at = jnp.arange(length, dtype=jnp.int32)
    allowed = (ids[None, :] == ids[:, None]) & (at[None, :] <= at[:, None])
    score = jnp.einsum("qjd,kd->jqk", queries, keys, preferred_element_type=f32) * 0.125
    score = jnp.where(allowed[None], score, MASKED)
    row_top = jnp.max(score, -1, keepdims=True)
    exponent = jnp.exp(score - row_top)
    soft_weights = exponent / jnp.sum(exponent, -1, keepdims=True)
    soft_low = soft_weights.astype(bf16)
    attended = jnp.einsum("jqk,kd->qjd", soft_low, values, preferred_element_type=f32)
    attended = attended.reshape(length, QW).astype(bf16)

    heads_team = lax.all_gather(attended, RING, axis=0, tiled=False).reshape(2, 4 * length, QW)
    resid = (
        tokens_team.astype(f32)
        + matmul(heads_team[0], full_o[:QW])
        + matmul(heads_team[1], full_o[QW:])
    )
    inv_two = inverse_rms(resid)
    normed_two = (resid * inv_two * full_g2[None, :]).astype(bf16)
    gate_up_part = matmul(normed_two, gate_up)
    gate_part, up_part = gate_up_part[:, :LOCAL_FF], gate_up_part[:, LOCAL_FF:]
    sigmoid_gate = jax.nn.sigmoid(gate_part)
    hidden = (gate_part * sigmoid_gate * up_part).astype(bf16)
    grad_hidden = matmul_nt(grad_low_team, down)
    grad_gate = (
        grad_hidden * up_part * sigmoid_gate * (1.0 + gate_part * (1.0 - sigmoid_gate))
    ).astype(bf16)
    grad_up = (grad_hidden * gate_part * sigmoid_gate).astype(bf16)
    grad_gate_up = jnp.concatenate([grad_gate, grad_up], 1)
    grad_normed_part = matmul_nt(grad_gate_up, gate_up).astype(bf16)
    grad_normed_all = exchange(grad_normed_part.reshape(8, row_count, D), TEAM)
    grad_normed_two = jnp.sum(grad_normed_all.astype(f32), 0)
    out_part = matmul(hidden, down).astype(bf16)
    out_all = exchange(out_part.reshape(8, row_count, D), TEAM)
    resid_own = lax.dynamic_slice_in_dim(resid, team_index * row_count, row_count)
    mixed_out = (resid_own + jnp.sum(out_all.astype(f32), 0)).astype(bf16)

    grad_gate_up_w = matmul_tn(normed_two, grad_gate_up).astype(bf16)
    grad_down_w = matmul_tn(hidden, grad_low_team).astype(bf16)
    wide_sums = exchange(grad_gate_up_w.reshape(16, 8 * ROWS, 2 * LOCAL_FF), PLANE)
    wide_sums = jnp.sum(wide_sums.astype(f32), 0).astype(bf16)
    wide_sums = exchange(wide_sums.reshape(8, ROWS, 2 * LOCAL_FF), TEAM).astype(f32)
    grad_w_gate = from_team(wide_sums[:, :, :LOCAL_FF])
    grad_w_up = from_team(wide_sums[:, :, LOCAL_FF:])
    down_sums = exchange(grad_down_w.reshape(16, UNIT_PAD, D), PLANE)
    grad_w_down = jnp.sum(down_sums.astype(f32), 0)[:UNIT]

    inv_two_own = inverse_rms(resid_own)
    grad_g2 = jnp.sum(grad_normed_two * resid_own * inv_two_own, 0)
    grad_resid = grad_output + norm_back(resid_own, inv_two_own, full_g2[None, :], grad_normed_two)

    grad_attn = grad_resid.astype(bf16)
    grad_attn_seq = in_order(grad_attn, lax.ppermute(grad_attn, "xh", SWAP), first)
    heads_own = lax.dynamic_slice_in_dim(heads_team, team_index * row_count, row_count, 1)
    grad_o_w = jnp.concatenate(
        [matmul_tn(heads_own[0], grad_attn), matmul_tn(heads_own[1], grad_attn)], 0
    ).astype(bf16)
    own_o = lax.dynamic_slice_in_dim(full_o, xh * QW, QW)
    grad_mixed = matmul_nt(grad_attn_seq, own_o).astype(bf16).reshape(length, GROUP, HEAD)
    grad_soft = jnp.einsum("qjd,kd->jqk", grad_mixed, values, preferred_element_type=f32)
    row_centre = jnp.sum(soft_weights * grad_soft, -1, keepdims=True)
    grad_score = (soft_weights * (grad_soft - row_centre)).astype(bf16)
    grad_query = jnp.einsum("jqk,kd->qjd", grad_score, keys, preferred_element_type=f32) * 0.125
    grad_keys = jnp.einsum("jqk,qjd->kd", grad_score, queries, preferred_element_type=f32) * 0.125
    grad_values = jnp.einsum("jqk,qjd->kd", soft_low, grad_mixed, preferred_element_type=f32)
    grad_raw = jnp.concatenate(
        [
            rotate(grad_query, cos_table, -sin_table).reshape(length, QW).astype(bf16),
            rotate(grad_keys, cos_table[:, 0], -sin_table[:, 0]).astype(bf16),
            grad_values.astype(bf16),
        ],
        1,
    )
    grad_qkv_w = matmul_tn(normed_one, grad_raw).astype(bf16)
    grad_bias = jnp.sum(grad_raw.astype(f32), 0)
    grad_normed_one = matmul_nt(grad_raw, w_qkv)
    grad_g1 = jnp.sum(grad_normed_one * source * inv_one, 0)
    to_partner = lax.dynamic_slice_in_dim(grad_normed_one, (1 - xh) * row_count, row_count)
    kept = lax.dynamic_slice_in_dim(grad_normed_one, xh * row_count, row_count)
    kept = kept + lax.ppermute(to_partner.astype(bf16), "xh", SWAP).astype(f32)
    source_own = tokens.astype(f32)
    input_grad = grad_resid + norm_back(
        source_own, inverse_rms(source_own), full_g1[None, :], kept
    )

    zero = jnp.zeros((D,), f32)
    small_bq = lax.dynamic_update_slice_in_dim(zero, grad_bias[:QW], xh * QW, 0)
    zero = jnp.zeros((128,), f32)
    small_bv = lax.dynamic_update_slice_in_dim(zero, grad_bias[QW + HEAD :], xh * HEAD, 0)
    small_out = jnp.concatenate(
        [
            jnp.broadcast_to(grad_bias[None, QW : QW + HEAD], (128, HEAD)),
            small_bq.reshape(128, ROWS),
            small_bv.reshape(128, 1),
            grad_g1.reshape(128, ROWS),
            grad_g2.reshape(128, ROWS),
        ],
        1,
    )
    small_out = jnp.pad(small_out, ((0, 0), (0, BLOCK - small_out.shape[1])))
    small_out = small_out.reshape(32, 2, 2, BLOCK).transpose(1, 0, 2, 3)
    small_out = jnp.where(core == 0, small_out, small_out[::-1]).reshape(128, 1, BLOCK)
    grad_blocks = matmul_tn(spread, grad_qkv_w).reshape(128, 8, BLOCK)
    grad_blocks = jnp.where(
        jnp.arange(8, dtype=jnp.int32)[None, :, None] == ROWS, small_out, grad_blocks
    )
    grad_o_blocks = matmul_tn(spread, grad_o_w).reshape(128, 8, D)

    def core_sum(array):
        low = array.astype(bf16)
        other = lax.ppermute(low[64:], "c", SWAP)
        return (low[:64].astype(f32) + other.astype(f32)).astype(bf16)

    o_sums = jnp.sum(exchange(core_sum(grad_o_blocks), SAME_CORE).astype(f32), 0)
    sums = exchange(core_sum(grad_blocks), SAME_CORE).astype(f32)
    sums = jnp.sum(sums.reshape(32, 2, 8, BLOCK), 0)
    grad_w_o = o_sums[:ROWS]
    grad_w_q = jnp.concatenate([sums[0, :ROWS, :QW], sums[1, :ROWS, :QW]], 1)
    grad_w_k = jnp.concatenate([sums[g, :ROWS, QW : QW + HEAD] for g in range(2)], 1)
    grad_w_v = jnp.concatenate([sums[g, :ROWS, QW + HEAD :] for g in range(2)], 1)
    grad_b_k = sums[:, ROWS, :HEAD].reshape(128)
    small_sums = jnp.sum(sums[:, ROWS, HEAD : HEAD + 22], 0)
    return (
        mixed_out,
        input_grad,
        grad_w_q,
        grad_w_k,
        grad_w_v,
        small_sums[0:7],
        grad_b_k,
        small_sums[7:8],
        grad_w_o,
        small_sums[8:15],
        grad_w_gate,
        grad_w_up,
        grad_w_down,
        small_sums[15:22],
    )


def solution(mesh):
    grid = Mesh(mesh.devices.reshape(4, 4, 2, 2, 2), ALL)
    rows = P(ALL, None)
    flat = P(ALL)
    in_specs = (
        rows,
        P(("z", "y", "xl", "c"), None),
        flat,
        flat,
        P(),
        rows,
        rows,
        rows,
        flat,
        flat,
        flat,
        rows,
        flat,
        rows,
        rows,
        rows,
        flat,
        rows,
    )
    out_specs = (rows, rows, rows, rows, rows, flat, P(), flat, rows, flat, rows, rows, rows, flat)
    return jax.shard_map(shards, mesh=grid, in_specs=in_specs, out_specs=out_specs, check_vma=False)
```

time: 3600 us -> 409 us (0.11)
  blocking collectives: 2270 us -> 12.9 us
  waiting for transfers between devices: 807 us -> 187 us
  starting transfers between devices: 234 us -> 53.6 us
  local copies, waits for them, and re-layouts: 172 us -> 46.1 us
    unnamed x4 -> x0, blocking collectives: 1640 us -> none
    all_gather x5 -> x4, waiting for transfers between devices: 797 us -> 116 us  [the longest x1 48.7 us: shards(): wide = lax.all_gather(wide, PLANE, axis=0, tiled=True)]
    all_gather x2 -> x0, blocking collectives: 625 us -> none  [the longest x1 313 us: shards(): lax.all_gather(w_k, ('dp', 'seq'), axis=0, tiled=True)]
    unnamed x60 -> x0, starting transfers between devices: 221 us -> none
    unnamed x192 -> x113, local copies, waits for them, and re-layouts: 169 us -> 7.46 us
    all_to_all x0 -> x8, waiting for transfers between devices: none -> 67.9 us  [exchange(): return lax.all_to_all(array, axes, split_axis=0, concat_axis=0, tiled=True)]
    all_to_all x0 -> x8, starting transfers between devices: none -> 46.5 us  [exchange(): return lax.all_to_all(array, axes, split_axis=0, concat_axis=0, tiled=True)]
    dot_general x26 -> x21, matrix products: 81.3 us -> 58.2 us  [the longest x6 17.6 us: matmul(): return jnp.dot(left, right, preferred_element_type=f32)]
  transfers between devices with their start and end apart: 69 -> 18, of which waited for: 6 -> 14; matrix products, arithmetic and copies ran while one was open for 21% -> 25% of each run, Pallas kernels for 0% -> 0%
where the time goes in v1:
time: 409 us; the launch traced here: 401 us
  waiting for transfers between devices  187 us (46%)
  matrix products  60.2 us (15%)
  starting transfers between devices  53.6 us (13%)
  local copies, waits for them, and re-layouts  46.1 us (11%)
  other arithmetic  25.1 us (6%)
  between operations  16.6 us (4%)
  blocking collectives  12.9 us (3%)
    all_to_all x8, waiting for transfers between devices, exchange(): return lax.all_to_all(array, axes, split_axis=0, concat_axis=0, tiled=True)  67.9 us
    all_gather x1, waiting for transfers between devices, shards(): wide = lax.all_gather(wide, PLANE, axis=0, tiled=True)  48.7 us
    all_to_all x8, starting transfers between devices, exchange(): return lax.all_to_all(array, axes, split_axis=0, concat_axis=0, tiled=True)  46.5 us
    all_gather x1, waiting for transfers between devices, shards(): down = lax.all_gather(down, PLANE, axis=0, tiled=True)  33.3 us
    all_gather x1, waiting for transfers between devices, shards(): both_team = lax.all_gather(both, RING, axis=0, tiled=False)  27.6 us
    dot_general x6, matrix products, matmul(): return jnp.dot(left, right, preferred_element_type=f32)  17.6 us
    dot_general x4, matrix products, matmul_nt(): lax.dot_general(left, right, (((1,), (1,)), ((), ())), preferred_element_...  17.5 us
    dot_general x6, matrix products, matmul_tn(): lax.dot_general(left, right, (((0,), (0,)), ((), ())), preferred_element_...  16 us
  transfers between devices with their start and end apart: 18, of which 14 were waited for; matrix products, arithmetic and copies ran while one was open for 25% of the time, Pallas kernels for 0%

profile of v1, /device:TPU:0, one launch (start us, length us, event | category | flops | bytes accessed | tf_op | source)
XLA Modules:
  0.0 401.0 jit_solution(16250433436735848874)
XLA Ops:
  13.3 11.6 %all-to-all-start = ((bf16[64,8,576]{2,1,0:T(8,128)(2,1)}), bf16[64,8,576]{2,1,0:T(8,128)(2,1)S(1)}, u32[]{:S(2)}, u32[]{:S(2)}) async-start(bf16[64,8,576]{2,1,0:T(8,128)(2,1)} %bitcast.5), calls=%async_computation | async-start | bytes 1310720 | tf_op jit(solution)/shard_map/all_to_all | solution.py:46
  25.0 3.2 collective-permute-start
  28.2 12.9 %all-to-all-done = bf16[64,8,576]{2,1,0:T(8,128)(2,1)S(1)} async-done(((bf16[64,8,576]{2,1,0:T(8,128)(2,1)}), bf16[64,8,576]{2,1,0:T(8,128)(2,1)S(1)}, u32[]{:S(2)}, u32[]{:S(2)}) %all-to-all-start) | async-done | bytes 589856 | tf_op jit(solution)/shard_map/all_to_all | solution.py:46
  56.9 12.9 %all_to_all.45 = bf16[8,7,2176]{2,1,0:T(8,128)(2,1)S(1)} all-to-all(bf16[8,7,2176]{2,1,0:T(8,128)(2,1)S(1)} %pad_maximum_fusion.5), channel_id=1, replica_groups=mesh['z'=4,'y'=4,'xl'=2,'c'=2,'xh'=2] {'xl','c','xh'}, dimensions={0} | all-to-all | bytes 487424 | tf_op jit(solution)/shard_map/all_to_all | solution.py:46
  71.7 6.0 %all-gather.6.cloned.1.call-done = bf16[8,256,448]{1,2,0:T(8,128)(2,1)} async-done(((bf16[1,256,448]{1,2,0:T(8,128)(2,1)}), bf16[8,256,448]{1,2,0:T(8,128)(2,1)}) %all-gather.6.cloned.1.call-update) | async-done | bytes 1835024 | tf_op jit(solution)/shard_map/all_gather | solution.py:200
  79.5 27.6 %all-gather.12.cloned.1.call-done = bf16[1024,1792]{1,0:T(8,128)(2,1)} async-done(((bf16[128,1792]{1,0:T(8,128)(2,1)}), bf16[1024,1792]{1,0:T(8,128)(2,1)}) %all-gather.12.cloned.1.call-update) | async-done | bytes 3670032 | tf_op jit(solution)/shard_map/all_gather | solution.py:163
  107.1 4.1 %copy.106 = bf16[2,2,2,128,1792]{4,3,2,1,0:T(8,128)(2,1)} copy(bf16[2,2,2,128,1792]{4,3,1,0,2:T(8,128)(2,1)} %bitcast.165) | data formatting | bytes 7340032 | tf_op jit(solution)/shard_map/transpose | solution.py:164
  111.1 48.7 %all-gather.8.cloned.1.call-done = bf16[896,2176]{1,0:T(8,128)(2,1)} async-done(((bf16[56,2176]{1,0:T(8,128)(2,1)}), bf16[896,2176]{1,0:T(8,128)(2,1)}) %all-gather.8.cloned.1.call-update) | async-done | bytes 3899408 | tf_op jit(solution)/shard_map/all_gather | solution.py:172
  166.8 4.8 %fusion.7 = f32[1024,1280]{1,0:T(8,128)} fusion(bf16[896,2176]{1,0:T(8,128)(2,1)S(1)} %copy-done.11, f32[1024,896]{1,0:T(8,128)S(1)} %get-tuple-element.76, f32[896]{0:T(1024)S(1)} %mul.403, f32[1024]{0:T(1024)S(1)} %add_rsqrt_fusion), kind=kOutput, calls=%fused_computation.21 | convolution fusion | flops 2351562752 | bytes 11214848 | tf_op jit(solution)/shard_map/dot_general | solution.py:34
  171.6 33.3 %all-gather.10.cloned.1.call-done = bf16[640,896]{1,0:T(8,128)(2,1)} async-done(((bf16[40,896]{1,0:T(8,128)(2,1)}), bf16[640,896]{1,0:T(8,128)(2,1)}) %all-gather.10.cloned.1.call-update) | async-done | bytes 1146896 | tf_op jit(solution)/shard_map/all_gather | solution.py:176
  204.9 7.0 %multiply_convert_fusion.2 = (bf16[1024,640]{1,0:T(8,128)(2,1)S(1)}, bf16[1024,640]{1,0:T(8,128)(2,1)}, bf16[1024,640]{1,0:T(8,128)(2,1)S(1)}) fusion(f32[1024,1280]{1,0:T(8,128)} %fusion.7, bf16[640,896]{1,0:T(8,128)(2,1)} %all-gather.10.cloned.1.call-done, bf16[1024,1792]{1,0:T(8,128)(2,1)} %bitcast.159), kind=kOutput, calls=%fused_computation.15 | convolution fusion | flops 1184890880 | bytes 12156928 | tf_op jit(solution)/shard_map/dot_general | solution.py:38
  214.4 4.9 %all-to-all-start.8 = ((bf16[16,40,896]{2,1,0:T(8,128)(2,1)}), bf16[16,40,896]{2,1,0:T(8,128)(2,1)S(1)}, u32[]{:S(2)}, u32[]{:S(2)}) async-start(bf16[16,40,896]{2,1,0:T(8,128)(2,1)} %bitcast.42), calls=%async_computation.8 | async-start | bytes 2293760 | tf_op jit(solution)/shard_map/all_to_all | solution.py:46
  219.4 6.2 %fusion.18 = bf16[1024,896]{1,0:T(8,128)(2,1)} fusion(bf16[896,2176]{1,0:T(8,128)(2,1)} %all-gather.8.cloned.1.call-done, bf16[1024,640]{1,0:T(8,128)(2,1)} %get-tuple-element.21, bf16[1024,640]{1,0:T(8,128)(2,1)S(1)} %get-tuple-element.20), kind=kOutput, calls=%fused_computation.37 | convolution fusion | flops 2354970624 | bytes 6750208 | tf_op jit(solution)/shard_map/dot_general | solution.py:38
  225.5 11.2 %all-to-all-done.8 = bf16[16,40,896]{2,1,0:T(8,128)(2,1)S(1)} async-done(((bf16[16,40,896]{2,1,0:T(8,128)(2,1)}), bf16[16,40,896]{2,1,0:T(8,128)(2,1)S(1)}, u32[]{:S(2)}, u32[]{:S(2)}) %all-to-all-start.8) | async-done | bytes 1146912 | tf_op jit(solution)/shard_map/all_to_all | solution.py:46
  236.7 4.7 %all-to-all-start.3 = ((bf16[8,128,896]{2,1,0:T(8,128)(2,1)}), bf16[8,128,896]{2,1,0:T(8,128)(2,1)}, u32[]{:S(2)}, u32[]{:S(2)}) async-start(bf16[8,128,896]{2,1,0:T(8,128)(2,1)} %bitcast.170), calls=%async_computation.3 | async-start | bytes 3670016 | tf_op jit(solution)/shard_map/all_to_all | solution.py:46
  244.2 5.0 %reshape.439 = bf16[2,1024,448]{1,0,2:T(2,128)(2,1)} reshape(bf16[8,256,448]{1,0,2:T(8,128)(2,1)} %copy.126) | data formatting | bytes 3670016 | tf_op jit(solution)/shard_map/reshape | solution.py:200
  249.2 4.3 %convolution_convert_fusion.1 = bf16[1024,896]{1,0:T(8,128)(2,1)} fusion(bf16[1024,640]{1,0:T(8,128)(2,1)} %copy-done.54, bf16[640,896]{1,0:T(8,128)(2,1)S(1)} %copy-done.48), kind=kOutput, calls=%fused_computation.39 | convolution fusion | flops 1175322624 | bytes 4292608 | tf_op jit(solution)/shard_map/dot_general | solution.py:34
  253.5 11.8 %all-to-all-done.3 = bf16[8,128,896]{2,1,0:T(8,128)(2,1)} async-done(((bf16[8,128,896]{2,1,0:T(8,128)(2,1)}), bf16[8,128,896]{2,1,0:T(8,128)(2,1)}, u32[]{:S(2)}, u32[]{:S(2)}) %all-to-all-start.3) | async-done | bytes 1835040 | tf_op jit(solution)/shard_map/all_to_all | solution.py:46
  265.2 3.6 all-to-all-start.2
  271.3 2.7 slice.274
  274.7 5.9 %convolution_convert_fusion = bf16[896,1280]{1,0:T(8,128)(2,1)} fusion(bf16[1024,640]{1,0:T(8,128)(2,1)} %get-tuple-element.21, bf16[1024,640]{1,0:T(8,128)(2,1)} %copy-done.55, f32[1024,896]{1,0:T(8,128)S(1)} %copy-done.5, f32[896]{0:T(1024)S(1)} %mul.403, f32[1024]{0:T(1024)S(1)} %copy-done.39), kind=kOutput, calls=%fused_computation.10 | convolution fusion | flops 2357952512 | bytes 8592896 | tf_op jit(solution)/shard_map/dot_general | solution.py:42
  284.4 8.2 %all-to-all-done.2 = bf16[8,128,896]{2,1,0:T(8,128)(2,1)S(1)} async-done(((bf16[8,128,896]{2,1,0:T(8,128)(2,1)}), bf16[8,128,896]{2,1,0:T(8,128)(2,1)S(1)}, u32[]{:S(2)}, u32[]{:S(2)}) %all-to-all-start.2) | async-done | bytes 1835040 | tf_op jit(solution)/shard_map/all_to_all | solution.py:46
  293.8 3.7 all-to-all-start.6
  316.0 2.6 fusion.39
  320.7 2.8 fusion.44
  326.9 4.4 %fusion.4 = bf16[128,8,576]{2,1,0:T(8,128)(2,1)} fusion(s32[1024]{0:T(1024)S(1)} %copy-done.37, bf16[128,576]{1,0:T(8,128)(2,1)S(1)} %broadcast_in_dim.57, pred[8]{0:T(512)(128)(4,1)S(1)} %copy-done.53, f32[896]{0:T(1024)S(1)} %mul.375, f32[256]{0:T(256)S(1)} %copy-done.45, bf16[256,64]{0,1:T(8,128)(2,1)S(1)} %copy-done.31, ...), kind=kOutput, calls=%fused_computation.13 | convolution fusion | flops 1328013312 | bytes 2089481 | tf_op jit(solution)/shard_map/dot_general | solution.py:42
  336.3 3.5 all-to-all-start.7
  341.8 3.7 all-to-all-done.7
  348.7 9.4 %all-to-all-start.4 = ((bf16[64,8,576]{2,1,0:T(8,128)(2,1)}), bf16[64,8,576]{2,1,0:T(8,128)(2,1)S(1)}, u32[]{:S(2)}, u32[]{:S(2)}) async-start(bf16[64,8,576]{2,1,0:T(8,128)(2,1)} %add_convert_fusion), calls=%async_computation.4 | async-start | bytes 1310720 | tf_op jit(solution)/shard_map/all_to_all | solution.py:46
  363.9 8.4 %all-to-all-done.4 = bf16[64,8,576]{2,1,0:T(8,128)(2,1)S(1)} async-done(((bf16[64,8,576]{2,1,0:T(8,128)(2,1)}), bf16[64,8,576]{2,1,0:T(8,128)(2,1)S(1)}, u32[]{:S(2)}, u32[]{:S(2)}) %all-to-all-start.4) | async-done | bytes 589856 | tf_op jit(solution)/shard_map/all_to_all | solution.py:46
  372.3 5.0 %all-to-all-start.5 = ((bf16[64,8,896]{2,1,0:T(8,128)(2,1)}), bf16[64,8,896]{2,1,0:T(8,128)(2,1)S(1)}, u32[]{:S(2)}, u32[]{:S(2)}) async-start(bf16[64,8,896]{2,1,0:T(8,128)(2,1)} %fusion.11), calls=%async_computation.5 | async-start | bytes 1835008 | tf_op jit(solution)/shard_map/all_to_all | solution.py:46
  381.5 11.8 %all-to-all-done.5 = bf16[64,8,896]{2,1,0:T(8,128)(2,1)S(1)} async-done(((bf16[64,8,896]{2,1,0:T(8,128)(2,1)}), bf16[64,8,896]{2,1,0:T(8,128)(2,1)S(1)}, u32[]{:S(2)}, u32[]{:S(2)}) %all-to-all-start.5) | async-done | bytes 917536 | tf_op jit(solution)/shard_map/all_to_all | solution.py:46
  (269 shorter events, 88.8 us)
Async XLA Ops:
  7.2 17.8 %copy-start.6 = (bf16[128,896]{1,0:T(8,128)(2,1)S(1)}, bf16[128,896]{1,0:T(8,128)(2,1)}, u32[]{:S(2)}) copy-start(bf16[128,896]{1,0:T(8,128)(2,1)} %param.18) | copy-start | bytes 688132
  13.3 28.2 %copy-start.34 = (s32[1,256]{1,0:T(1,128)S(1)}, s32[1,256]{1,0:T(1,128)}, u32[]{:S(2)}) copy-start(s32[1,256]{1,0:T(1,128)} %param.19) | copy-start | bytes 3076
  13.3 27.9 %all-to-all-start = ((bf16[64,8,576]{2,1,0:T(8,128)(2,1)}), bf16[64,8,576]{2,1,0:T(8,128)(2,1)S(1)}, u32[]{:S(2)}, u32[]{:S(2)}) async-start(bf16[64,8,576]{2,1,0:T(8,128)(2,1)} %bitcast.5), calls=%async_computation | async-start | bytes 1310720 | tf_op jit(solution)/shard_map/all_to_all | solution.py:46
  24.9 52.8 %all-gather.6.cloned.1.call-start = ((), (), s32[]{:S(2)}) async-start(), calls=%async_computation.9 | async-start | bytes 2064384 | tf_op jit(solution)/shard_map/all_gather | solution.py:200
  25.0 17.2 %collective-permute-start = (bf16[128,896]{1,0:T(8,128)(2,1)S(1)}, bf16[128,896]{1,0:T(8,128)(2,1)S(1)}, u32[]{:S(2)}, u32[]{:S(2)}) collective-permute-start(bf16[128,896]{1,0:T(8,128)(2,1)S(1)} %copy-done.6), channel_id=1, source_target_pairs={{0,1},{1,0},{2,3},{3,2},{4,5},{5,4},{6,7},{7,6},{8,9},{9,8},{10,11... | collective-permute-start | bytes 688136 | tf_op jit(solution)/shard_map/ppermute | solution.py:178
  41.3 2.2 collective-permute-start.1
  41.4 5.5 %copy-start.35 = (s32[1024]{0:T(1024)}, s32[1024]{0:T(1024)S(1)}, u32[]{:S(2)}) copy-start(s32[1024]{0:T(1024)S(1)} %fusion.103) | copy-start | bytes 12292
  42.2 5.1 %copy-start.20 = (bf16[128,896]{1,0:T(8,128)(2,1)}, bf16[128,896]{1,0:T(8,128)(2,1)S(1)}, u32[]{:S(2)}) copy-start(bf16[128,896]{1,0:T(8,128)(2,1)S(1)} %collective-permute-done) | copy-start | bytes 688132
  42.4 4.9 %copy-start.44 = (f32[256]{0:T(256)}, f32[256]{0:T(256)S(1)}, u32[]{:S(2)}) copy-start(f32[256]{0:T(256)S(1)} %add_rsqrt_fusion.1) | copy-start | bytes 3076
  53.8 53.3 %all-gather.12.cloned.1.call-start = ((), (), s32[]{:S(2)}) async-start(), calls=%async_computation.12 | async-start | bytes 4128768 | tf_op jit(solution)/shard_map/all_gather | solution.py:163
  54.9 104.9 %all-gather.8.cloned.1.call-start = ((), (), s32[]{:S(2)}) async-start(), calls=%async_computation.10 | async-start | bytes 4143104 | tf_op jit(solution)/shard_map/all_gather | solution.py:172
  55.9 14.9 %copy-start.28 = (bf16[38,896]{1,0:T(8,128)(2,1)S(1)}, bf16[38,896]{1,0:T(8,128)(2,1)}, u32[]{:S(2)}) copy-start(bf16[38,896]{1,0:T(8,128)(2,1)} %param.33) | copy-start | bytes 204292
  70.6 134.3 %all-gather.10.cloned.1.call-start = ((), (), s32[]{:S(2)}) async-start(), calls=%async_computation.11 | async-start | bytes 1218560 | tf_op jit(solution)/shard_map/all_gather | solution.py:176
  204.9 7.0 %copy-start.1 = (bf16[2,2,2,128,1792]{4,3,2,1,0:T(8,128)(2,1)S(1)}, bf16[2,2,2,128,1792]{4,3,2,1,0:T(8,128)(2,1)}, u32[]{:S(2)}) copy-start(bf16[2,2,2,128,1792]{4,3,2,1,0:T(8,128)(2,1)} %copy.106) | copy-start | bytes 11010052
  211.8 7.5 %copy-start.55 = (bf16[1024,640]{1,0:T(8,128)(2,1)}, bf16[1024,640]{1,0:T(8,128)(2,1)S(1)}, u32[]{:S(2)}) copy-start(bf16[1024,640]{1,0:T(8,128)(2,1)S(1)} %get-tuple-element.20) | copy-start | bytes 3932164
  214.4 22.3 %all-to-all-start.8 = ((bf16[16,40,896]{2,1,0:T(8,128)(2,1)}), bf16[16,40,896]{2,1,0:T(8,128)(2,1)S(1)}, u32[]{:S(2)}, u32[]{:S(2)}) async-start(bf16[16,40,896]{2,1,0:T(8,128)(2,1)} %bitcast.42), calls=%async_computation.8 | async-start | bytes 2293760 | tf_op jit(solution)/shard_map/all_to_all | solution.py:46
  236.7 5.2 %copy-start.2 = (bf16[8,256,448]{1,2,0:T(8,128)(2,1)S(1)}, bf16[8,256,448]{1,2,0:T(8,128)(2,1)}, u32[]{:S(2)}) copy-start(bf16[8,256,448]{1,2,0:T(8,128)(2,1)} %all-gather.6.cloned.1.call-done) | copy-start | bytes 5505028
  236.7 28.5 %all-to-all-start.3 = ((bf16[8,128,896]{2,1,0:T(8,128)(2,1)}), bf16[8,128,896]{2,1,0:T(8,128)(2,1)}, u32[]{:S(2)}, u32[]{:S(2)}) async-start(bf16[8,128,896]{2,1,0:T(8,128)(2,1)} %bitcast.170), calls=%async_computation.3 | async-start | bytes 3670016 | tf_op jit(solution)/shard_map/all_to_all | solution.py:46
  244.2 5.0 %copy-start.48 = (bf16[640,896]{1,0:T(8,128)(2,1)S(1)}, bf16[640,896]{1,0:T(8,128)(2,1)}, u32[]{:S(2)}) copy-start(bf16[640,896]{1,0:T(8,128)(2,1)} %all-gather.10.cloned.1.call-done) | copy-start | bytes 3440644
  265.2 27.3 %all-to-all-start.2 = ((bf16[8,128,896]{2,1,0:T(8,128)(2,1)}), bf16[8,128,896]{2,1,0:T(8,128)(2,1)S(1)}, u32[]{:S(2)}, u32[]{:S(2)}) async-start(bf16[8,128,896]{2,1,0:T(8,128)(2,1)} %bitcast.171), calls=%async_computation.2 | async-start | bytes 3670016 | tf_op jit(solution)/shard_map/all_to_all | solution.py:46
  268.8 5.2 %copy-start.5 = (f32[1024,896]{1,0:T(8,128)S(1)}, f32[1024,896]{1,0:T(8,128)}, u32[]{:S(2)}) copy-start(f32[1024,896]{1,0:T(8,128)} %copy-done.4) | copy-start | bytes 11010052
  274.7 8.5 %copy-start.40 = (f32[128]{0:T(128)}, f32[128]{0:T(128)S(1)}, u32[]{:S(2)}) copy-start(f32[128]{0:T(128)S(1)} %get-tuple-element.72) | copy-start | bytes 1540
  293.8 41.4 %all-to-all-start.6 = ((bf16[16,56,1280]{2,1,0:T(8,128)(2,1)}), bf16[16,56,1280]{2,1,0:T(8,128)(2,1)S(1)}, u32[]{:S(2)}, u32[]{:S(2)}) async-start(bf16[16,56,1280]{2,1,0:T(8,128)(2,1)} %bitcast.169), calls=%async_computation.6 | async-start | bytes 4587520 | tf_op jit(solution)/shard_map/all_to_all | solution.py:46
  301.6 9.1 %collective-permute-start.2 = (bf16[128,896]{1,0:T(8,128)(2,1)S(1)}, bf16[128,896]{1,0:T(8,128)(2,1)S(1)}, u32[]{:S(2)}, u32[]{:S(2)}) collective-permute-start(bf16[128,896]{1,0:T(8,128)(2,1)S(1)} %get-tuple-element.18), channel_id=1, source_target_pairs={{0,1},{1,0},{2,3},{3,2},{4,5},{5,4},{6,7},{7,6},{8,9},{9,8},{10,11... | collective-permute-start | bytes 688136 | tf_op jit(solution)/shard_map/ppermute | solution.py:241
  308.9 52.7 %collective-permute-start.5 = (bf16[64,8,896]{2,1,0:T(8,128)(2,1)}, bf16[64,8,896]{2,1,0:T(8,128)(2,1)}, u32[]{:S(2)}, u32[]{:S(2)}) collective-permute-start(bf16[64,8,896]{2,1,0:T(8,128)(2,1)} %slice_bitcast_fusion), channel_id=1, source_target_pairs={{0,2},{2,0},{1,3},{3,1},{4,6},{6,4},{5,7},{7,5},{8,10},{10,8},{9,1... | collective-permute-start | bytes 2752520 | tf_op jit(solution)/shard_map/ppermute | solution.py:299
  325.5 8.5 %collective-permute-start.3 = (bf16[128,896]{1,0:T(8,128)(2,1)S(1)}, bf16[128,896]{1,0:T(8,128)(2,1)S(1)}, u32[]{:S(2)}, u32[]{:S(2)}) collective-permute-start(bf16[128,896]{1,0:T(8,128)(2,1)S(1)} %dynamic-slice_convert_fusion), channel_id=1, source_target_pairs={{0,1},{1,0},{2,3},{3,2},{4,5},{5,4},{6,7},{7,6},{8,9},{9,8},{10,11... | collective-permute-start | bytes 688136 | tf_op jit(solution)/shard_map/ppermute | solution.py:268
  333.4 6.5 %copy-start.8 = (f32[128,896]{1,0:T(8,128)S(1)}, f32[128,896]{1,0:T(8,128)}, u32[]{:S(2)}) copy-start(f32[128,896]{1,0:T(8,128)} %get-tuple-element.19) | copy-start | bytes 1376260
  333.4 13.2 %collective-permute-start.4 = (bf16[64,8,576]{2,1,0:T(8,128)(2,1)}, bf16[64,8,576]{2,1,0:T(8,128)(2,1)}, u32[]{:S(2)}, u32[]{:S(2)}) collective-permute-start(bf16[64,8,576]{2,1,0:T(8,128)(2,1)} %slice.280), channel_id=1, source_target_pairs={{0,2},{2,0},{1,3},{3,1},{4,6},{6,4},{5,7},{7,5},{8,10},{10,8},{9,1... | collective-permute-start | bytes 1769480 | tf_op jit(solution)/shard_map/ppermute | solution.py:299
  336.3 10.3 %copy-start.12 = (bf16[128,8,576]{2,1,0:T(8,128)(2,1)S(1)}, bf16[128,8,576]{2,1,0:T(8,128)(2,1)}, u32[]{:S(2)}) copy-start(bf16[128,8,576]{2,1,0:T(8,128)(2,1)} %fusion.4) | copy-start | bytes 3538948
  336.3 9.2 %all-to-all-start.7 = ((bf16[8,7,1280]{2,1,0:T(8,128)(2,1)}), bf16[8,7,1280]{2,1,0:T(8,128)(2,1)S(1)}, u32[]{:S(2)}, u32[]{:S(2)}) async-start(bf16[8,7,1280]{2,1,0:T(8,128)(2,1)} %reshape.441), calls=%async_computation.7 | async-start | bytes 327680 | tf_op jit(solution)/shard_map/all_to_all | solution.py:46
  348.7 23.7 %all-to-all-start.4 = ((bf16[64,8,576]{2,1,0:T(8,128)(2,1)}), bf16[64,8,576]{2,1,0:T(8,128)(2,1)S(1)}, u32[]{:S(2)}, u32[]{:S(2)}) async-start(bf16[64,8,576]{2,1,0:T(8,128)(2,1)} %add_convert_fusion), calls=%async_computation.4 | async-start | bytes 1310720 | tf_op jit(solution)/shard_map/all_to_all | solution.py:46
  372.3 20.9 %all-to-all-start.5 = ((bf16[64,8,896]{2,1,0:T(8,128)(2,1)}), bf16[64,8,896]{2,1,0:T(8,128)(2,1)S(1)}, u32[]{:S(2)}, u32[]{:S(2)}) async-start(bf16[64,8,896]{2,1,0:T(8,128)(2,1)} %fusion.11), calls=%async_computation.5 | async-start | bytes 1835008 | tf_op jit(solution)/shard_map/all_to_all | solution.py:46
  (42 other events, 101.2 us)
Sparse Core Ops, SparseCore 0:
  53.9 23.7 all-gather.5
  79.9 27.0 all-gather.11
  109.2 50.5 all-gather.7
  162.4 42.4 all-gather.9
